TPU v7x, 128 devices: a whole 4x4x4 slice. The times are simulated.
128 devices in a mesh: expert: 32 (over y, x, core), tensor: 4 (over z).
Axes of the slice: x: 4, y: 4, z: 4, core: 2. Of those that a mesh axis runs over, the one named last changes fastest.
Arguments:
- block_input: bfloat16 [4096, 2880], P('expert'), may hold values from -6 to 6
- out_cotangent: bfloat16 [4096, 2880], P('expert'), may hold values from -6 to 6
- seq_lengths: int32 [32, 4], P('expert'), may hold values from 1 to 64, 128 in all within a row
- route_ids: int32 [4096, 4], P('expert'), may hold values from 0 to 31, all different within a row; in each aligned block of 128 rows (0 to 127, 128 to 255, ...) at most 32 rows name the same one
- attn_gain: float32 [2880], replicated, may hold values from 0.5 to 1.5
- w_query: bfloat16 [2880, 4096], P('expert', 'tensor'), may hold values from -0.109375 to 0.109375
- w_key: bfloat16 [2880, 512], P('expert', 'tensor'), may hold values from -0.109375 to 0.109375
- w_value: bfloat16 [2880, 512], P('expert', 'tensor'), may hold values from -0.109375 to 0.109375
- b_query: float32 [4096], P('tensor'), may hold values from -1.2 to 1.2
- b_key: float32 [512], P('tensor'), may hold values from -1.2 to 1.2
- b_value: float32 [512], P('tensor'), may hold values from -1.2 to 1.2
- sink_logits: float32 [64], P('tensor'), may hold values from -4 to 4
- w_output: bfloat16 [4096, 2880], P('tensor', 'expert'), may hold values from -0.25 to 0.25
- b_output: float32 [2880], replicated, may hold values from -1.2 to 1.2
- ffn_gain: float32 [2880], replicated, may hold values from 0.5 to 1.5
- w_router: float32 [2880, 32], replicated, may hold values from -0.0546875 to 0.0546875
- b_router: float32 [32], replicated, may hold values from -3 to 3
- w_gate: bfloat16 [32, 2880, 2880], P('expert', None, 'tensor'), may hold values from -0.109375 to 0.109375
- w_up: bfloat16 [32, 2880, 2880], P('expert', None, 'tensor'), may hold values from -0.109375 to 0.109375
- b_gate: float32 [32, 2880], P('expert', 'tensor'), may hold values from -0.6 to 0.6
- b_up: float32 [32, 2880], P('expert', 'tensor'), may hold values from -0.6 to 0.6
- w_down: bfloat16 [32, 2880, 2880], P('expert', 'tensor'), may hold values from -0.109375 to 0.109375
- b_down: float32 [32, 2880], P('expert'), may hold values from -0.6 to 0.6
Outputs:
- block_output: bfloat16 [4096, 2880], P('expert')
- input_grad: float32 [4096, 2880], P('expert')
- attn_gain_grad: float32 [2880], replicated
- w_query_grad: float32 [2880, 4096], P('expert', 'tensor')
- w_key_grad: float32 [2880, 512], P('expert', 'tensor')
- w_value_grad: float32 [2880, 512], P('expert', 'tensor')
- b_query_grad: float32 [4096], P('tensor')
- b_key_grad: float32 [512], P('tensor')
- b_value_grad: float32 [512], P('tensor')
- sink_grad: float32 [64], P('tensor')
- w_output_grad: float32 [4096, 2880], P('tensor', 'expert')
- b_output_grad: float32 [2880], replicated
- ffn_gain_grad: float32 [2880], replicated
- w_router_grad: float32 [2880, 32], replicated
- b_router_grad: float32 [32], replicated
- w_gate_grad: float32 [32, 2880, 2880], P('expert', None, 'tensor')
- w_up_grad: float32 [32, 2880, 2880], P('expert', None, 'tensor')
- b_gate_grad: float32 [32, 2880], P('expert', 'tensor')
- b_up_grad: float32 [32, 2880], P('expert', 'tensor')
- w_down_grad: float32 [32, 2880, 2880], P('expert', 'tensor')
- b_down_grad: float32 [32, 2880], P('expert')
Inputs may be any that keep to these rules, and one draw needn't show every extreme that they name: `seq_lengths`: each row lists in order the lengths of the 4 sequences packed into one device's 128 tokens; they sum to 128 and the longest is exactly 64. `route_ids`: each row names 4 different experts; within the rows of one device no expert is named more than 32 times, and in some device's rows an expert is named exactly 32 times.
All inputs are finite; a program needn't handle non-finite values.
Results may differ from a plain program's by a relative error of at most 0.034.
Values may be sent and summed in bfloat16 or wider, within the bound.
No kernel may reach another device: no remote copies, remote signals or barrier semaphores. Data moves between devices by JAX's collectives and lax.ppermute only.
A program may use at most 256 MiB of HBM per device.

v0:
```python
import jax
import jax.numpy as jnp
from jax import lax
from jax.sharding import PartitionSpec as P

HD = 64


EPSILON = 1e-05
ROPE_BASE = 150000.0
CLAMP_LIMIT = 7.0
GLU_SLOPE = 1.702
MASKED = -1e30
PRECISE = lax.Precision.HIGHEST


def rms_norm(values, gain_vec):
    return (
        values * lax.rsqrt(jnp.mean(values * values, axis=-1, keepdims=True) + EPSILON) * gain_vec
    )


def layout(lengths, tok_count):
    seq_ends = jnp.cumsum(lengths)
    tok_index = jnp.arange(tok_count, dtype=jnp.int32)
    is_past = tok_index[:, None] >= seq_ends[None, :]
    segment = jnp.sum(is_past.astype(jnp.int32), axis=1)
    offset = jnp.sum(jnp.where(is_past, lengths[None, :], 0), axis=1)
    return (segment, tok_index - offset)


def rotation(position, head_size):
    half_size = head_size // 2
    frequency = ROPE_BASE ** (-(jnp.arange(half_size).astype(jnp.float32) * 2.0 / head_size))
    angles = position.astype(jnp.float32)[:, None] * frequency[None, :]
    return (jnp.cos(angles), jnp.sin(angles))


def rotate(values, cosine, sine_table):
    half_size = values.shape[-1] // 2
    first = values[..., :half_size]
    second = values[..., half_size:]
    cos_cols = cosine[:, None, :]
    sin_cols = sine_table[:, None, :]
    return jnp.concatenate(
        [first * cos_cols - second * sin_cols, second * cos_cols + first * sin_cols], axis=-1
    )


def activate(gate_lin, up_lin):
    gate_soft = CLAMP_LIMIT * jnp.tanh(gate_lin / CLAMP_LIMIT)
    up_soft = CLAMP_LIMIT * jnp.tanh(up_lin / CLAMP_LIMIT)
    return (up_soft + 1.0) * gate_soft * jax.nn.sigmoid(GLU_SLOPE * gate_soft)


def column_sum(values):
    return jnp.dot(
        jnp.ones((1, values.shape[0]), values.dtype), values, preferred_element_type=jnp.float32
    )[0]


def block_scores(queries, key_rows, query_seg, query_pos, key_seg, key_pos):
    score_scale = queries.shape[-1] ** (-0.5)
    scores = (
        jnp.einsum("bhgd,khd->hgbk", queries, key_rows, preferred_element_type=jnp.float32)
        * score_scale
    )
    allowed = (query_seg[:, None] == key_seg[None, :]) & (key_pos[None, :] <= query_pos[:, None])
    return (scores, allowed)


def attend_forward(
    queries, key_rows, value_rows, sink_table, query_seg, query_pos, key_seg, key_pos
):
    scores, allowed = block_scores(queries, key_rows, query_seg, query_pos, key_seg, key_pos)
    scores = jnp.where(allowed, scores, MASKED)
    sink_col = sink_table[:, :, None]
    row_max = jnp.maximum(jnp.max(scores, axis=-1), sink_col)
    denom_sum = jnp.sum(jnp.exp(scores - row_max[..., None]), axis=-1) + jnp.exp(sink_col - row_max)
    logsum = row_max + jnp.log(denom_sum)
    probability = jnp.exp(scores - logsum[..., None]).astype(jnp.bfloat16)
    attended = jnp.einsum(
        "hgbk,khd->bhgd", probability, value_rows, preferred_element_type=jnp.float32
    )
    return (attended, logsum)


def attend_backward(
    queries,
    key_rows,
    value_rows,
    sink_table,
    logsum,
    grad_attended,
    query_seg,
    query_pos,
    key_seg,
    key_pos,
):
    score_scale = queries.shape[-1] ** (-0.5)
    scores, allowed = block_scores(queries, key_rows, query_seg, query_pos, key_seg, key_pos)
    probability = jnp.where(allowed, jnp.exp(scores - logsum[..., None]), 0.0)
    grad_probs = jnp.einsum(
        "bhgd,khd->hgbk", grad_attended, value_rows, preferred_element_type=jnp.float32
    )
    delta_sum = jnp.sum(probability * grad_probs, axis=-1)
    grad_scores = (probability * (grad_probs - delta_sum[..., None])).astype(jnp.bfloat16)
    grad_query = (
        jnp.einsum("hgbk,khd->bhgd", grad_scores, key_rows, preferred_element_type=jnp.float32)
        * score_scale
    )
    grad_keys = (
        jnp.einsum("hgbk,bhgd->khd", grad_scores, queries, preferred_element_type=jnp.float32)
        * score_scale
    )
    grad_values = jnp.einsum(
        "hgbk,bhgd->khd",
        probability.astype(jnp.bfloat16),
        grad_attended,
        preferred_element_type=jnp.float32,
    )
    grad_sinks = -jnp.sum(jnp.exp(sink_table[:, :, None] - logsum) * delta_sum, axis=-1)
    return (grad_query, grad_keys, grad_values, grad_sinks)


def to_owners(row_vals, destination, expert_count, capacity):
    feat_width = row_vals.shape[1]
    buffer = (
        jnp.zeros((expert_count * capacity, feat_width), row_vals.dtype)
        .at[destination]
        .set(row_vals)
    )
    moved_rows = lax.all_to_all(
        buffer.reshape(expert_count, capacity, feat_width),
        "expert",
        split_axis=0,
        concat_axis=0,
        tiled=True,
    )
    return moved_rows.reshape(expert_count * capacity, feat_width)


def to_sources(partial_rows, bias_vec, expert_count, capacity):
    feat_width = partial_rows.shape[1]
    summed = lax.psum(partial_rows, "tensor")
    slice_start = 0
    if bias_vec is not None:
        summed = summed + bias_vec
    sent_rows = summed.astype(jnp.bfloat16).reshape(expert_count, capacity, summed.shape[1])
    returned = lax.all_to_all(sent_rows, "expert", split_axis=0, concat_axis=0, tiled=True)
    return returned.reshape(expert_count * capacity, feat_width)


def on_device(
    block_input,
    out_cotangent,
    seq_lengths,
    route_ids,
    attn_gain,
    w_query,
    w_key,
    w_value,
    b_query,
    b_key,
    b_value,
    sink_logits,
    w_output,
    b_output,
    ffn_gain,
    w_router,
    b_router,
    w_gate,
    w_up,
    b_gate,
    b_up,
    w_down,
    b_down,
):
    tok_count, feat_width = block_input.shape
    heads_here = sink_logits.shape[0]
    head_size = HD
    kv_here = b_key.shape[0] // head_size
    group_size = heads_here // kv_here
    expert_count = w_router.shape[1]
    route_count = route_ids.shape[1]
    capacity = 2 * tok_count * route_count // expert_count
    block_rows = min(tok_count, 512)
    block_count = tok_count // block_rows
    segment, position = layout(seq_lengths[0], tok_count)
    cosine, sine_table = rotation(position, head_size)
    block_seg = segment.reshape(block_count, block_rows)
    block_pos = position.reshape(block_count, block_rows)
    inputs = block_input.astype(jnp.float32)
    normed, norm_one_back = jax.vjp(rms_norm, inputs, attn_gain)
    normed_low = normed.astype(jnp.bfloat16)
    full_query, full_key, full_value, full_output = (
        lax.all_gather(w_query, "expert", axis=0, tiled=True),
        lax.all_gather(w_key, "expert", axis=0, tiled=True),
        lax.all_gather(w_value, "expert", axis=0, tiled=True),
        lax.all_gather(w_output, "expert", axis=1, tiled=True),
    )
    query_lin = jnp.dot(normed_low, full_query, preferred_element_type=jnp.float32) + b_query
    key_lin = jnp.dot(normed_low, full_key, preferred_element_type=jnp.float32) + b_key
    value_lin = jnp.dot(normed_low, full_value, preferred_element_type=jnp.float32) + b_value
    query_low = rotate(
        query_lin.reshape(tok_count, heads_here, head_size), cosine, sine_table
    ).astype(jnp.bfloat16)
    query_low = query_low.reshape(block_count, block_rows, kv_here, group_size, head_size)
    key_low = rotate(key_lin.reshape(tok_count, kv_here, head_size), cosine, sine_table).astype(
        jnp.bfloat16
    )
    value_low = value_lin.reshape(tok_count, kv_here, head_size).astype(jnp.bfloat16)
    sink_table = sink_logits.reshape(kv_here, group_size)

    def forward_block(item_tuple):
        return attend_forward(
            item_tuple[0],
            key_low,
            value_low,
            sink_table,
            item_tuple[1],
            item_tuple[2],
            segment,
            position,
        )

    attended, logsum = lax.map(forward_block, (query_low, block_seg, block_pos))
    attn_low = attended.reshape(tok_count, heads_here * head_size).astype(jnp.bfloat16)
    attn_total = lax.psum(
        jnp.dot(attn_low, full_output, preferred_element_type=jnp.float32), "tensor"
    )
    residual = inputs + attn_total + b_output
    normed_two, norm_two_back = jax.vjp(rms_norm, residual, ffn_gain)
    ffn_low = normed_two.astype(jnp.bfloat16)
    logits = jnp.dot(normed_two, w_router, precision=PRECISE) + b_router
    onehot = (
        route_ids[:, :, None] == jnp.arange(expert_count, dtype=jnp.int32)[None, None, :]
    ).astype(jnp.float32)
    chosen = jnp.sum(logits[:, None, :] * onehot, axis=-1)
    gate_probs = jax.nn.softmax(chosen, axis=-1)
    flat_hot = onehot.reshape(tok_count * route_count, expert_count)
    slot_index = jnp.sum((jnp.cumsum(flat_hot, axis=0) - flat_hot) * flat_hot, axis=1).astype(
        jnp.int32
    )
    destination = route_ids.reshape(-1) * capacity + slot_index
    rows_in = to_owners(
        jnp.repeat(ffn_low, route_count, axis=0), destination, expert_count, capacity
    )
    gate_lin = jnp.dot(rows_in, w_gate[0], preferred_element_type=jnp.float32) + b_gate[0]
    up_lin = jnp.dot(rows_in, w_up[0], preferred_element_type=jnp.float32) + b_up[0]
    hidden, act_back = jax.vjp(activate, gate_lin, up_lin)
    hidden_low = hidden.astype(jnp.bfloat16)
    returned = to_sources(
        jnp.dot(hidden_low, w_down[0], preferred_element_type=jnp.float32),
        b_down[0],
        expert_count,
        capacity,
    )
    expert_rows = returned[destination].reshape(tok_count, route_count, feat_width)
    mixed_out = jnp.sum(gate_probs[:, :, None] * expert_rows.astype(jnp.float32), axis=1)
    block_output = (residual + mixed_out).astype(jnp.bfloat16)
    cotangent = out_cotangent.astype(jnp.float32)
    grad_gates = jnp.sum(cotangent[:, None, :] * expert_rows.astype(jnp.float32), axis=-1)
    grad_rows = (
        (gate_probs[:, :, None] * cotangent[:, None, :])
        .astype(jnp.bfloat16)
        .reshape(tok_count * route_count, feat_width)
    )
    grad_owner = to_owners(grad_rows, destination, expert_count, capacity)
    b_down_grad = column_sum(grad_owner)[None, :]
    w_down_grad = jnp.dot(hidden_low.T, grad_owner, preferred_element_type=jnp.float32)[None]
    grad_hidden = jnp.dot(grad_owner, w_down[0].T, preferred_element_type=jnp.float32)
    grad_gate, grad_up = act_back(grad_hidden)
    grad_gate_low = grad_gate.astype(jnp.bfloat16)
    grad_up_low = grad_up.astype(jnp.bfloat16)
    b_gate_grad = column_sum(grad_gate_low)[None, :]
    b_up_grad = column_sum(grad_up_low)[None, :]
    w_gate_grad = jnp.dot(rows_in.T, grad_gate_low, preferred_element_type=jnp.float32)[None]
    w_up_grad = jnp.dot(rows_in.T, grad_up_low, preferred_element_type=jnp.float32)[None]
    grad_rows_in = jnp.dot(
        grad_gate_low, w_gate[0].T, preferred_element_type=jnp.float32
    ) + jnp.dot(grad_up_low, w_up[0].T, preferred_element_type=jnp.float32)
    grad_back = to_sources(grad_rows_in, None, expert_count, capacity)
    grad_expert = jnp.sum(
        grad_back[destination].reshape(tok_count, route_count, feat_width).astype(jnp.float32),
        axis=1,
    )
    grad_chosen = gate_probs * (
        grad_gates - jnp.sum(gate_probs * grad_gates, axis=-1, keepdims=True)
    )
    grad_logits = jnp.sum(grad_chosen[:, :, None] * onehot, axis=1)
    router_part = jnp.dot(normed_two.T, grad_logits, precision=PRECISE)
    router_bias_part = jnp.sum(grad_logits, axis=0)
    grad_normed_two = grad_expert + jnp.dot(grad_logits, w_router.T, precision=PRECISE)
    grad_resid_norm, ffn_gain_part = norm_two_back(grad_normed_two)
    grad_resid = cotangent + grad_resid_norm
    output_bias_part = jnp.sum(grad_resid, axis=0)
    grad_total_low = grad_resid.astype(jnp.bfloat16)
    grad_attn = jnp.dot(grad_total_low, full_output.T, preferred_element_type=jnp.float32).astype(
        jnp.bfloat16
    )
    grad_attn = grad_attn.reshape(block_count, block_rows, kv_here, group_size, head_size)

    def backward_block(carry, item_tuple):
        grad_query, grad_keys, grad_values, grad_sinks = attend_backward(
            item_tuple[0],
            key_low,
            value_low,
            sink_table,
            item_tuple[1],
            item_tuple[2],
            item_tuple[3],
            item_tuple[4],
            segment,
            position,
        )
        return ((carry[0] + grad_keys, carry[1] + grad_values, carry[2] + grad_sinks), grad_query)

    start_carry = (
        jnp.zeros((tok_count, kv_here, head_size), jnp.float32),
        jnp.zeros((tok_count, kv_here, head_size), jnp.float32),
        jnp.zeros((kv_here, group_size), jnp.float32),
    )
    carried, grad_query_rot = lax.scan(
        backward_block, start_carry, (query_low, logsum, grad_attn, block_seg, block_pos)
    )
    grad_key_rot, grad_value_sum, grad_sink_table = carried
    grad_query_low = (
        rotate(grad_query_rot.reshape(tok_count, heads_here, head_size), cosine, -sine_table)
        .reshape(tok_count, heads_here * head_size)
        .astype(jnp.bfloat16)
    )
    grad_key_low = (
        rotate(grad_key_rot, cosine, -sine_table)
        .reshape(tok_count, kv_here * head_size)
        .astype(jnp.bfloat16)
    )
    grad_value_low = grad_value_sum.reshape(tok_count, kv_here * head_size).astype(jnp.bfloat16)
    grad_normed_part = jnp.dot(grad_query_low, full_query.T, preferred_element_type=jnp.float32)
    grad_normed_part = grad_normed_part + jnp.dot(
        grad_key_low, full_key.T, preferred_element_type=jnp.float32
    )
    grad_normed_part = grad_normed_part + jnp.dot(
        grad_value_low, full_value.T, preferred_element_type=jnp.float32
    )
    grad_normed = lax.psum(grad_normed_part.astype(jnp.bfloat16), "tensor").astype(jnp.float32)
    grad_inputs_norm, attn_gain_part = norm_one_back(grad_normed)
    input_grad = grad_resid + grad_inputs_norm
    query_full = jnp.dot(normed_low.T, grad_query_low, preferred_element_type=jnp.float32)
    key_full = jnp.dot(normed_low.T, grad_key_low, preferred_element_type=jnp.float32)
    value_full = jnp.dot(normed_low.T, grad_value_low, preferred_element_type=jnp.float32)
    output_full = jnp.dot(attn_low.T, grad_total_low, preferred_element_type=jnp.float32)
    w_query_grad, w_key_grad, w_value_grad, w_output_grad = (
        lax.psum_scatter(
            query_full.astype(jnp.bfloat16), "expert", scatter_dimension=0, tiled=True
        ).astype(jnp.float32),
        lax.psum_scatter(
            key_full.astype(jnp.bfloat16), "expert", scatter_dimension=0, tiled=True
        ).astype(jnp.float32),
        lax.psum_scatter(
            value_full.astype(jnp.bfloat16), "expert", scatter_dimension=0, tiled=True
        ).astype(jnp.float32),
        lax.psum_scatter(
            output_full.astype(jnp.bfloat16), "expert", scatter_dimension=1, tiled=True
        ).astype(jnp.float32),
    )
    summed_small = (
        lax.psum(attn_gain_part.astype(jnp.bfloat16), "expert").astype(jnp.float32),
        lax.psum(column_sum(grad_query_low).astype(jnp.bfloat16), "expert").astype(jnp.float32),
        lax.psum(column_sum(grad_key_low).astype(jnp.bfloat16), "expert").astype(jnp.float32),
        lax.psum(column_sum(grad_value_low).astype(jnp.bfloat16), "expert").astype(jnp.float32),
        lax.psum(grad_sink_table.reshape(-1).astype(jnp.bfloat16), "expert").astype(jnp.float32),
        lax.psum(output_bias_part.astype(jnp.bfloat16), "expert").astype(jnp.float32),
        lax.psum(ffn_gain_part.astype(jnp.bfloat16), "expert").astype(jnp.float32),
        lax.psum(router_part.astype(jnp.bfloat16), "expert").astype(jnp.float32),
        lax.psum(router_bias_part.astype(jnp.bfloat16), "expert").astype(jnp.float32),
    )
    return (
        block_output,
        input_grad,
        summed_small[0],
        w_query_grad,
        w_key_grad,
        w_value_grad,
        summed_small[1],
        summed_small[2],
        summed_small[3],
        summed_small[4],
        w_output_grad,
        summed_small[5],
        summed_small[6],
        summed_small[7],
        summed_small[8],
        w_gate_grad,
        w_up_grad,
        b_gate_grad,
        b_up_grad,
        w_down_grad,
        b_down_grad,
    )


def solution(mesh):
    in_specs = (
        P("expert", None),
        P("expert", None),
        P("expert", None),
        P("expert", None),
        P(),
        P("expert", "tensor"),
        P("expert", "tensor"),
        P("expert", "tensor"),
        P("tensor"),
        P("tensor"),
        P("tensor"),
        P("tensor"),
        P("tensor", "expert"),
        P(),
        P(),
        P(),
        P(),
        P("expert", None, "tensor"),
        P("expert", None, "tensor"),
        P("expert", "tensor"),
        P("expert", "tensor"),
        P("expert", "tensor", None),
        P("expert", None),
    )
    out_specs = (
        P("expert", None),
        P("expert", None),
        P(),
        P("expert", "tensor"),
        P("expert", "tensor"),
        P("expert", "tensor"),
        P("tensor"),
        P("tensor"),
        P("tensor"),
        P("tensor"),
        P("tensor", "expert"),
        P(),
        P(),
        P(),
        P(),
        P("expert", None, "tensor"),
        P("expert", None, "tensor"),
        P("expert", "tensor"),
        P("expert", "tensor"),
        P("expert", "tensor", None),
        P("expert", None),
    )
    return jax.shard_map(
        on_device, mesh=mesh, in_specs=in_specs, out_specs=out_specs, check_vma=False
    )
```

profile of v0, /device:TPU:32, one launch (start us, length us, event | category | flops | bytes accessed | tf_op | source)
XLA Modules:
  0.0 1383.6 jit_solution(15642378542518449337)
XLA Ops:
  8.8 25.8 %all-gather.1 = bf16[32,90,128]{2,1,0:T(8,128)(2,1)S(1)} all-gather(bf16[1,90,128]{2,1,0:T(8,128)(2,1)} %bitcast.201), channel_id=1, replica_groups=mesh['expert'=32,'tensor'=4] {'expert'}, dimensions={0}, use_global_device_ids=true | all-gather | bytes 760320 | tf_op jit(solution)/shard_map/all_gather | solution.py:198
  35.6 24.3 %all-gather = bf16[32,90,128]{2,1,0:T(8,128)(2,1)S(1)} all-gather(bf16[1,90,128]{2,1,0:T(8,128)(2,1)} %bitcast.202), channel_id=1, replica_groups=mesh['expert'=32,'tensor'=4] {'expert'}, dimensions={0}, use_global_device_ids=true | all-gather | bytes 760320 | tf_op jit(solution)/shard_map/all_gather | solution.py:199
  64.0 8.4 reshape.529
  79.1 34.5 %all-gather.9.cloned.1.call-done = bf16[32,90,1024]{2,1,0:T(8,128)(2,1)} async-done(((bf16[1,90,1024]{2,1,0:T(8,128)(2,1)}), bf16[32,90,1024]{2,1,0:T(8,128)(2,1)}) %all-gather.9.cloned.1.call-update) | async-done | bytes 5898256 | tf_op jit(solution)/shard_map/all_gather | solution.py:200
  113.5 8.2 reshape.531
  133.4 7.8 mul.453
  141.2 34.0 %all-reduce.16.cloned.1.call-done = f32[128,2880]{0,1:T(8,128)} async-done(((f32[128,2880]{0,1:T(8,128)}), f32[128,2880]{0,1:T(8,128)}) %all-reduce.16.cloned.1.call-update) | async-done | bytes 1474576 | tf_op jit(solution)/shard_map/psum | solution.py:229
  179.6 10.8 scatter_custom_fusion.1
  206.8 9.6 scatter_custom_fusion
  216.4 56.2 %all-to-all-done.2 = bf16[32,32,2880]{2,1,0:T(8,128)(2,1)} async-done(((bf16[32,32,2880]{2,1,0:T(8,128)(2,1)}), bf16[32,32,2880]{2,1,0:T(8,128)(2,1)}, u32[]{:S(2)}, u32[]{:S(2)}) %all-to-all-start.2) | async-done | bytes 5898272 | tf_op jit(solution)/shard_map/all_to_all | solution.py:133
  277.9 10.3 fusion.4
  288.2 64.0 %all-to-all-done = bf16[32,32,2880]{2,1,0:T(8,128)(2,1)} async-done(((bf16[32,32,2880]{2,1,0:T(8,128)(2,1)}), bf16[32,32,2880]{2,1,0:T(8,128)(2,1)}, u32[]{:S(2)}, u32[]{:S(2)}) %all-to-all-start) | async-done | bytes 5898272 | tf_op jit(solution)/shard_map/all_to_all | solution.py:133
  352.2 8.2 fusion.13
  360.5 13.6 multiply_convert_fusion.2
  375.6 8.6 fusion.6
  384.3 11.9 fusion.8
  396.2 10.5 convolution_add_fusion
  406.7 368.6 %all-reduce.23 = bf16[1024,2880]{0,1:T(8,128)(2,1)} all-reduce(f32[1024,2880]{0,1:T(8,128)} %convolution_add_fusion), channel_id=1, replica_groups=mesh['expert'=32,'tensor'=4] {'tensor'}, use_global_device_ids=true, to_apply=%region_18.19 | all-reduce | flops 2949120 | bytes 17694720 | tf_op jit(solution)/shard_map/psum | solution.py:145
  775.3 8.5 copy.127
  791.2 7.6 add_convert_fusion
  798.8 8.5 copy.123
  807.3 58.4 %all-to-all-done.3 = bf16[32,32,2880]{2,1,0:T(8,128)(2,1)} async-done(((bf16[32,32,2880]{2,1,0:T(8,128)(2,1)}), bf16[32,32,2880]{2,1,0:T(8,128)(2,1)}, u32[]{:S(2)}, u32[]{:S(2)}) %all-to-all-start.3) | async-done | bytes 5898272 | tf_op jit(solution)/shard_map/all_to_all | solution.py:150
  881.4 10.1 convolution_bitcast_fusion
  891.5 9.8 convolution_bitcast_fusion.1
  901.3 10.9 convolution_bitcast_fusion.2
  912.2 10.2 gather_fusion.1
  945.5 10.3 gather_fusion
  962.3 9.1 multiply_reduce_fusion
  1000.0 92.5 %fusion.100 = (bf16[96,1024]{1,0:T(8,128)(2,1)S(1)}, bf16[96,128]{1,0:T(8,128)(2,1)S(1)}, bf16[96,128]{1,0:T(8,128)(2,1)S(1)}, bf16[1024,96]{0,1:T(8,128)(2,1)S(1)}) fusion(bf16[2880,1024]{1,0:T(8,128)(2,1)} %convolution_convert_fusion.1, bf16[2880,128]{1,0:T(8,128)(2,1)S(1)} %convolution_convert_fusion.3, ...), kind=kCustom, calls=%all-reduce-scatter.4 | all-reduce-scatter fusion | flops 7077889 | bytes 13713920
  1127.9 68.1 %all-reduce.22.cloned.1.call-done = bf16[2880,32]{0,1:T(8,128)(2,1)} async-done(((bf16[2880,32]{0,1:T(8,128)(2,1)}), bf16[2880,32]{0,1:T(8,128)(2,1)}) %all-reduce.22.cloned.1.call-update) | async-done | bytes 184336 | tf_op jit(solution)/shard_map/psum | solution.py:375
  1209.7 30.6 %all-reduce.20.cloned.1.call-done = bf16[128,2880]{0,1:T(8,128)(2,1)} async-done(((bf16[128,2880]{0,1:T(8,128)(2,1)}), bf16[128,2880]{0,1:T(8,128)(2,1)}) %all-reduce.20.cloned.1.call-update) | async-done | bytes 737296 | tf_op jit(solution)/shard_map/psum | solution.py:346
  1242.4 126.8 %all-reduce.8 = (bf16[2880]{0:T(1024)(128)(2,1)S(1)}, bf16[1024]{0:T(1024)(128)(2,1)S(1)}, bf16[128]{0:T(256)(128)(2,1)S(1)}, bf16[128]{0:T(256)(128)(2,1)S(1)},...) all-reduce(bf16[2880]{0:T(1024)(128)(2,1)S(1)} %get-tuple-element.8, ...), channel_id=1, replica_groups=mesh['expert'=32,'tensor'=4] {'expert'}, use_global_device_ids=true, to_apply=%region_28.29 | all-reduce | flops 9968 | bytes 39872 | tf_op jit(solution)/shard_map/psum | solution.py:368
  (318 shorter events, 190.5 us)
Async XLA Ops:
  7.2 169.9 %copy-start = (f32[2880,32]{0,1:T(8,128)S(1)}, f32[2880,32]{0,1:T(8,128)}, u32[]{:S(2)}) copy-start(f32[2880,32]{0,1:T(8,128)} %param.38) | copy-start | bytes 1105924
  7.2 52.9 %copy-start.65 = (s32[1,4]{1,0:T(1,128)S(1)}, s32[1,4]{1,0:T(1,128)}, u32[]{:S(2)}) copy-start(s32[1,4]{1,0:T(1,128)} %param.25) | copy-start | bytes 52
  7.2 53.2 %copy-start.1 = (bf16[128,2880]{0,1:T(8,128)(2,1)S(1)}, bf16[128,2880]{0,1:T(8,128)(2,1)}, u32[]{:S(2)}) copy-start(bf16[128,2880]{0,1:T(8,128)(2,1)} %param.23) | copy-start | bytes 2211844
  7.2 56.8 %all-gather.7.cloned.1.call-start = ((), (), s32[]{:S(2)}) async-start(), calls=%async_computation.8 | async-start | bytes 6488064 | tf_op jit(solution)/shard_map/all_gather | solution.py:197
  7.3 54.9 %copy-start.17 = (f32[2880]{0:T(1024)S(1)}, f32[2880]{0:T(1024)}, u32[]{:S(2)}) copy-start(f32[2880]{0:T(1024)} %param.27) | copy-start | bytes 34564
  7.3 54.9 %copy-start.66 = (f32[128]{0:T(128)S(1)}, f32[128]{0:T(128)}, u32[]{:S(2)}) copy-start(f32[128]{0:T(128)} %param.32) | copy-start | bytes 1540
  8.0 105.6 %all-gather.9.cloned.1.call-start = ((), (), s32[]{:S(2)}) async-start(), calls=%async_computation.9 | async-start | bytes 6488064 | tf_op jit(solution)/shard_map/all_gather | solution.py:200
  8.7 166.5 %all-reduce.16.cloned.1.call-start = ((), (), s32[]{:S(2)}) async-start(), calls=%async_computation.4 | async-start | bytes 2949120 | tf_op jit(solution)/shard_map/psum | solution.py:229
  35.6 42.4 %copy-start.50 = (f32[2,8]{1,0:T(2,128)}, f32[2,8]{1,0:T(2,128)S(1)}, u32[]{:S(2)}) copy-start(f32[2,8]{1,0:T(2,128)S(1)} %max.24) | copy-start | bytes 196
  79.1 42.7 %copy-start.12 = (bf16[2,64,8,128]{3,1,2,0:T(8,128)(2,1)}, bf16[2,64,8,128]{3,1,2,0:T(8,128)(2,1)S(1)}, u32[]{:S(2)}) copy-start(bf16[2,64,8,128]{3,1,2,0:T(8,128)(2,1)S(1)} %convolution_convert_fusion.6) | copy-start | bytes 786436
  133.4 41.8 %copy-start.48 = (f32[2880]{0:T(1024)S(1)}, f32[2880]{0:T(1024)}, u32[]{:S(2)}) copy-start(f32[2880]{0:T(1024)} %param.36) | copy-start | bytes 34564
  141.2 35.9 %copy-start.59 = (f32[32]{0:T(128)S(1)}, f32[32]{0:T(128)}, u32[]{:S(2)}) copy-start(f32[32]{0:T(128)} %param.39) | copy-start | bytes 388
  190.3 82.2 %all-to-all-start.2 = ((bf16[32,32,2880]{2,1,0:T(8,128)(2,1)}), bf16[32,32,2880]{2,1,0:T(8,128)(2,1)}, u32[]{:S(2)}, u32[]{:S(2)}) async-start(bf16[32,32,2880]{2,1,0:T(8,128)(2,1)} %bitcast.174), calls=%async_computation.2 | async-start | bytes 12058624 | tf_op jit(solution)/shard_map/all_to_all | solution.py:133
  272.5 79.7 %all-to-all-start = ((bf16[32,32,2880]{2,1,0:T(8,128)(2,1)}), bf16[32,32,2880]{2,1,0:T(8,128)(2,1)}, u32[]{:S(2)}, u32[]{:S(2)}) async-start(bf16[32,32,2880]{2,1,0:T(8,128)(2,1)} %bitcast.175), calls=%async_computation | async-start | bytes 12058624 | tf_op jit(solution)/shard_map/all_to_all | solution.py:133
  277.6 513.6 %all-reduce.18.cloned.1.call-start = ((), (), s32[]{:S(2)}) async-start(), calls=%async_computation.5 | async-start | bytes 23592960 | tf_op jit(solution)/shard_map/psum | solution.py:145
  783.8 82.0 %all-to-all-start.3 = ((bf16[32,32,2880]{2,1,0:T(8,128)(2,1)}), bf16[32,32,2880]{2,1,0:T(8,128)(2,1)}, u32[]{:S(2)}, u32[]{:S(2)}) async-start(bf16[32,32,2880]{2,1,0:T(8,128)(2,1)} %bitcast.176), calls=%async_computation.3 | async-start | bytes 12058624 | tf_op jit(solution)/shard_map/all_to_all | solution.py:150
  865.8 79.7 %all-to-all-start.1 = ((bf16[32,32,2880]{2,1,0:T(8,128)(2,1)}), bf16[32,32,2880]{2,1,0:T(8,128)(2,1)}, u32[]{:S(2)}, u32[]{:S(2)}) async-start(bf16[32,32,2880]{2,1,0:T(8,128)(2,1)} %bitcast.173), calls=%async_computation.1 | async-start | bytes 12058624 | tf_op jit(solution)/shard_map/all_to_all | solution.py:150
  870.8 325.2 %all-reduce.22.cloned.1.call-start = ((), (), s32[]{:S(2)}) async-start(), calls=%async_computation.7 | async-start | bytes 376832 | tf_op jit(solution)/shard_map/psum | solution.py:375
  1093.2 104.5 %collective-permute-start.6 = (bf16[1024,96]{0,1:T(8,128)(2,1)S(1)}, bf16[1024,96]{0,1:T(8,128)(2,1)}, u32[]{:S(2)}, u32[]{:S(2)}) collective-permute-start(bf16[1024,96]{0,1:T(8,128)(2,1)S(1)} %get-tuple-element.124), channel_id=1, source_target_pairs={{0,4},{4,8},{8,12},{12,16},{16,20},{20,24},{24,28},{28,32},{32,36}... | collective-permute-start | bytes 589832
  1100.4 139.9 %all-reduce.20.cloned.1.call-start = ((), (), s32[]{:S(2)}) async-start(), calls=%async_computation.6 | async-start | bytes 1474560 | tf_op jit(solution)/shard_map/psum | solution.py:346
  1104.6 7.3 collective-permute-start.4
  1105.9 15.8 %collective-permute-start.2 = (bf16[96,128]{1,0:T(8,128)(2,1)S(1)}, bf16[96,128]{1,0:T(8,128)(2,1)S(1)}, u32[]{:S(2)}, u32[]{:S(2)}) collective-permute-start(bf16[96,128]{1,0:T(8,128)(2,1)S(1)} %get-tuple-element.122), channel_id=1, source_target_pairs={{0,4},{4,8},{8,12},{12,16},{16,20},{20,24},{24,28},{28,32},{32,36}... | collective-permute-start | bytes 73736
  1107.2 3.4 collective-permute-start.5
  1108.5 11.7 collective-permute-start.3
  1110.7 91.8 %collective-permute-start = (bf16[96,1024]{1,0:T(8,128)(2,1)S(1)}, bf16[96,1024]{1,0:T(8,128)(2,1)S(1)}, u32[]{:S(2)}, u32[]{:S(2)}) collective-permute-start(bf16[96,1024]{1,0:T(8,128)(2,1)S(1)} %get-tuple-element.121), channel_id=1, source_target_pairs={{0,4},{4,8},{8,12},{12,16},{16,20},{20,24},{24,28},{28,32},{32,36}... | collective-permute-start | bytes 589832
  1112.0 85.7 %collective-permute-start.7 = (bf16[1024,90]{0,1:T(8,128)(2,1)}, bf16[1024,90]{0,1:T(8,128)(2,1)}, u32[]{:S(2)}, u32[]{:S(2)}) collective-permute-start(bf16[1024,90]{0,1:T(8,128)(2,1)} %slice.56), channel_id=1, source_target_pairs={{0,8},{4,12},{8,16},{12,20},{16,24},{20,28},{24,32},{28,36},{32,40... | collective-permute-start | bytes 552968
  1120.2 122.2 %copy-start.45 = (bf16[2880]{0:T(1024)(128)(2,1)S(1)}, bf16[2880]{0:T(1024)(128)(2,1)}, u32[]{:S(2)}) copy-start(bf16[2880]{0:T(1024)(128)(2,1)} %get-tuple-element.125) | copy-start | bytes 17284
  1120.2 122.2 %copy-start.57 = (bf16[128]{0:T(256)(128)(2,1)S(1)}, bf16[128]{0:T(256)(128)(2,1)}, u32[]{:S(2)}) copy-start(bf16[128]{0:T(256)(128)(2,1)} %fusion.48) | copy-start | bytes 772
  1120.2 122.2 %copy-start.58 = (bf16[32]{0:T(256)(128)(2,1)S(1)}, bf16[32]{0:T(256)(128)(2,1)}, u32[]{:S(2)}) copy-start(bf16[32]{0:T(256)(128)(2,1)} %get-tuple-element.105) | copy-start | bytes 196
  1120.3 82.2 %collective-permute-start.1 = (bf16[90,1024]{1,0:T(8,128)(2,1)}, bf16[90,1024]{1,0:T(8,128)(2,1)S(1)}, u32[]{:S(2)}, u32[]{:S(2)}) collective-permute-start(bf16[90,1024]{1,0:T(8,128)(2,1)} %slice.53), channel_id=1, source_target_pairs={{0,8},{4,12},{8,16},{12,20},{16,24},{20,28},{24,32},{28,36},{32,40... | collective-permute-start | bytes 552968
  1125.1 248.7 %copy-start.61 = (f32[128]{0:T(128)S(1)}, f32[128]{0:T(128)}, u32[]{:S(2)}) copy-start(f32[128]{0:T(128)} %copy-done.60) | copy-start | bytes 1540
  1125.1 248.7 %copy-start.4 = (f32[128,2880]{0,1:T(8,128)S(1)}, f32[128,2880]{0,1:T(8,128)}, u32[]{:S(2)}) copy-start(f32[128,2880]{0,1:T(8,128)} %copy-done.3) | copy-start | bytes 4423684
  (65 other events, 501.4 us)
Sparse Core Ops, SparseCore 0:
  10.3 52.9 all-gather.6
  65.5 47.9 all-gather.8
  127.4 47.7 all-reduce.15
  384.4 380.3 all-reduce.17
  1100.5 95.4 all-reduce.21
  1198.2 42.0 all-reduce.19
where the time goes:
time: 1390 us; the launch traced here: 1380 us
  blocking collectives  638 us (46%)
  waiting for transfers between devices  353 us (25%)
  matrix products  145 us (10%)
  local copies, waits for them, and re-layouts  127 us (9%)
  other arithmetic  63.5 us (5%)
  starting transfers between devices  40.2 us (3%)
  between operations  16.3 us (1%)
    psum x1, blocking collectives, to_sources(): summed = lax.psum(partial_rows, 'tensor')  369 us
    psum x1, blocking collectives, on_device(): lax.psum(attn_gain_part.astype(jnp.bfloat16), 'expert').astype(jnp.float32)  127 us
    all_to_all x2, waiting for transfers between devices, to_owners(): lax.all_to_all(buffer.reshape(expert_count, capacity, feat_width), 'exper...  120 us
    unnamed x1, blocking collectives  92.5 us
    psum x1, waiting for transfers between devices, on_device(): lax.psum(router_part.astype(jnp.bfloat16), 'expert').astype(jnp.float32)  68.1 us
    all_to_all x2, waiting for transfers between devices, to_sources(): lax.all_to_all(sent_rows, 'expert', split_axis=0, concat_axis=0, tiled=True)  64.4 us
    unnamed x172, local copies, waits for them, and re-layouts  38.6 us
    all_gather x1, waiting for transfers between devices, on_device(): lax.all_gather(w_output, 'expert', axis=1, tiled=True)  34.5 us
  transfers between devices with their start and end apart: 18, of which 8 were waited for; matrix products, arithmetic and copies ran while one was open for 15% of the time, Pallas kernels for 0%

commit v1 on v0

v1 whole, which is shorter than its diff:
```python
import functools

import jax
import jax.numpy as jnp
from jax import lax
from jax.experimental import pallas as pl
from jax.experimental.pallas import tpu as pltpu
from jax.sharding import PartitionSpec as P

HD = 64
PAIR = 2 * HD
EPSILON = 1e-05
ROPE_BASE = 150000.0
CLAMP_LIMIT = 7.0
GLU_SLOPE = 1.702
MASKED = -1e30
PRECISE = lax.Precision.HIGHEST
LOW = jnp.bfloat16
F32 = jnp.float32
VMEM_BYTES = 56 * 1024 * 1024
NN = (((1,), (0,)), ((), ()))
NT = (((1,), (1,)), ((), ()))
TN = (((0,), (0,)), ((), ()))


def round_up(value, unit):
    return -(-value // unit) * unit


def dot(left, right, dims=NN):
    return lax.dot_general(left, right, dims, preferred_element_type=F32)


def split_low(values):
    high = values.astype(LOW)
    return high, (values - high.astype(F32)).astype(LOW)


def layout(lengths, tok_count):
    seq_ends = jnp.cumsum(lengths)
    tok_index = jnp.arange(tok_count, dtype=jnp.int32)
    is_past = tok_index[:, None] >= seq_ends[None, :]
    segment = jnp.sum(is_past.astype(jnp.int32), axis=1)
    offset = jnp.sum(jnp.where(is_past, lengths[None, :], 0), axis=1)
    return (segment, tok_index - offset)


def rope_tables(position):
    half = HD // 2
    frequency = ROPE_BASE ** (-(jnp.arange(half).astype(F32) * 2.0 / HD))
    angles = position.astype(F32)[:, None] * frequency[None, :]
    cosine, sine = jnp.cos(angles), jnp.sin(angles)
    return (
        jnp.concatenate([cosine] * 4, axis=1),
        jnp.concatenate([-sine, sine, -sine, sine], axis=1),
    )


def lane_index(shape):
    return lax.broadcasted_iota(jnp.int32, shape, len(shape) - 1)


def swap_halves(values):
    first = (lane_index(values.shape) % HD) < HD // 2
    return jnp.where(
        first, pltpu.roll(values, PAIR - HD // 2, 1), pltpu.roll(values, HD // 2, 1)
    )


def twin(values, which):
    turned = pltpu.roll(values, HD, 1)
    left = lane_index(values.shape) < HD
    return jnp.where(left, values, turned) if which == 0 else jnp.where(left, turned, values)


def attend_forward_kernel(
    sink_ref, qkv_ref, cos_ref, sin_ref, allowed_ref, out_ref, rot_ref, lse_ref
):
    tokens = qkv_ref.shape[0]
    heads = sink_ref.shape[0]
    key_at = heads * HD
    value_at = key_at + PAIR
    per_group = heads // 2
    cos, sin = cos_ref[...], sin_ref[...]
    allowed = allowed_ref[...] > 0.5
    left = lane_index((tokens, PAIR)) < HD
    lanes = lane_index((tokens, PAIR))

    def rope(values):
        return values * cos + swap_halves(values) * sin

    key = rope(qkv_ref[:, key_at:value_at])
    value = qkv_ref[:, value_at : value_at + PAIR]
    rot_ref[:, key_at:value_at] = key.astype(LOW)
    rot_ref[:, value_at : value_at + PAIR] = value.astype(LOW)
    keys = [twin(key, g).astype(LOW) for g in range(2)]
    values = [twin(value, g).astype(LOW) for g in range(2)]
    lse_all = jnp.zeros((tokens, PAIR), F32)
    for pair in range(heads // 2):
        cols = slice(pair * PAIR, (pair + 1) * PAIR)
        group = (2 * pair) // per_group
        query = rope(qkv_ref[:, cols])
        rot_ref[:, cols] = query.astype(LOW)
        outs = []
        for side in range(2):
            head = 2 * pair + side
            mine = left if side == 0 else jnp.logical_not(left)
            one = jnp.where(mine, query, 0.0).astype(LOW)
            scores = dot(one, keys[group], NT) * HD ** (-0.5)
            scores = jnp.where(allowed, scores, MASKED)
            sink = sink_ref[head]
            top = jnp.maximum(jnp.max(scores, axis=1, keepdims=True), sink)
            weights = jnp.exp(scores - top)
            denom = jnp.sum(weights, axis=1, keepdims=True) + jnp.exp(sink - top)
            lse = top + jnp.log(denom)
            lse_all = jnp.where(lanes == head, lse, lse_all)
            prob = (weights / denom).astype(LOW)
            outs.append(dot(prob, values[group]))
        out_ref[:, cols] = jnp.where(left, outs[0], outs[1]).astype(LOW)
    lse_ref[...] = lse_all


def attend_backward_kernel(
    sink_ref, rot_ref, grad_ref, lse_ref, cos_ref, sin_ref, allowed_ref, out_ref, sink_out_ref
):
    tokens = rot_ref.shape[0]
    heads = sink_ref.shape[0]
    key_at = heads * HD
    value_at = key_at + PAIR
    per_group = heads // 2
    scale = HD ** (-0.5)
    cos, sin = cos_ref[...], sin_ref[...]
    allowed = allowed_ref[...] > 0.5
    lanes = lane_index((tokens, PAIR))
    left = lanes < HD

    def turn_back(values):
        return values * cos - swap_halves(values) * sin

    key = rot_ref[:, key_at:value_at].astype(F32)
    value = rot_ref[:, value_at : value_at + PAIR].astype(F32)
    keys = [twin(key, g).astype(LOW) for g in range(2)]
    values = [twin(value, g).astype(LOW) for g in range(2)]
    key_sums = [jnp.zeros((tokens, PAIR), F32) for _ in range(2)]
    value_sums = [jnp.zeros((tokens, PAIR), F32) for _ in range(2)]
    sink_all = jnp.zeros((tokens, PAIR), F32)
    lse_all = lse_ref[...]
    for pair in range(heads // 2):
        cols = slice(pair * PAIR, (pair + 1) * PAIR)
        group = (2 * pair) // per_group
        query = rot_ref[:, cols].astype(F32)
        grad = grad_ref[:, cols].astype(F32)
        outs = []
        for side in range(2):
            head = 2 * pair + side
            mine = left if side == 0 else jnp.logical_not(left)
            one = jnp.where(mine, query, 0.0).astype(LOW)
            grad_one = jnp.where(mine, grad, 0.0).astype(LOW)
            lse = jnp.sum(jnp.where(lanes == head, lse_all, 0.0), axis=1, keepdims=True)
            scores = dot(one, keys[group], NT) * scale
            prob = jnp.where(allowed, jnp.exp(jnp.where(allowed, scores - lse, 0.0)), 0.0)
            grad_prob = dot(grad_one, values[group], NT)
            delta = jnp.sum(prob * grad_prob, axis=1, keepdims=True)
            grad_score = (prob * (grad_prob - delta)).astype(LOW)
            outs.append(dot(grad_score, keys[group]))
            key_sums[group] += dot(grad_score, one, TN)
            value_sums[group] += dot(prob.astype(LOW), grad_one, TN)
            sink_all = jnp.where(lanes == head, jnp.exp(sink_ref[head] - lse) * delta, sink_all)
        out_ref[:, cols] = turn_back(jnp.where(left, outs[0], outs[1]) * scale).astype(LOW)

    def fold(sums):
        both = [one + pltpu.roll(one, HD, 1) for one in sums]
        return jnp.where(left, both[0], both[1])

    out_ref[:, key_at:value_at] = turn_back(fold(key_sums) * scale).astype(LOW)
    out_ref[:, value_at : value_at + PAIR] = fold(value_sums).astype(LOW)
    sink_out_ref[...] = -jnp.sum(sink_all, axis=0, keepdims=True)


def kernel_params():
    return pltpu.CompilerParams(vmem_limit_bytes=VMEM_BYTES)


IN_VMEM = pl.BlockSpec(memory_space=pltpu.VMEM)
IN_SMEM = pl.BlockSpec(memory_space=pltpu.SMEM)


def attend_forward(sinks, qkv, cos, sin, allowed):
    tokens, width = qkv.shape
    heads = sinks.shape[0]
    return pl.pallas_call(
        attend_forward_kernel,
        out_shape=(
            jax.ShapeDtypeStruct((tokens, heads * HD), LOW),
            jax.ShapeDtypeStruct((tokens, width), LOW),
            jax.ShapeDtypeStruct((tokens, PAIR), F32),
        ),
        in_specs=[IN_SMEM] + [IN_VMEM] * 4,
        out_specs=(IN_VMEM,) * 3,
        compiler_params=kernel_params(),
        name="attend_forward",
    )(sinks, qkv, cos, sin, allowed)


def attend_backward(sinks, rotated, grad, lse, cos, sin, allowed):
    tokens, width = rotated.shape
    return pl.pallas_call(
        attend_backward_kernel,
        out_shape=(
            jax.ShapeDtypeStruct((tokens, width), LOW),
            jax.ShapeDtypeStruct((1, PAIR), F32),
        ),
        in_specs=[IN_SMEM] + [IN_VMEM] * 6,
        out_specs=(IN_VMEM,) * 2,
        compiler_params=kernel_params(),
        name="attend_backward",
    )(sinks, rotated, grad, lse, cos, sin, allowed)


def grad_hidden_kernel(rows_ref, down_ref, bias_ref, out_ref):
    rows = rows_ref[...]
    hidden = down_ref.shape[0]
    spare = out_ref.shape[1] - hidden
    out_ref[:, :hidden] = dot(rows, down_ref[...], NT)
    with_bias = jnp.sum(rows.astype(F32) * bias_ref[...], axis=1, keepdims=True)
    out_ref[:, hidden:] = jnp.broadcast_to(with_bias, (rows.shape[0], spare))


def grad_hidden_product(rows, down, bias):
    count, features = rows.shape
    hidden = down.shape[0]
    width = round_up(hidden + 1, 128)
    block = count // 4
    return pl.pallas_call(
        grad_hidden_kernel,
        grid=(count // block,),
        out_shape=jax.ShapeDtypeStruct((count, width), F32),
        in_specs=[
            pl.BlockSpec((block, features), lambda i: (i, 0)),
            pl.BlockSpec((hidden, features), lambda i: (0, 0)),
            pl.BlockSpec((1, features), lambda i: (0, 0)),
        ],
        out_specs=pl.BlockSpec((block, width), lambda i: (i, 0)),
        compiler_params=kernel_params(),
        cost_estimate=pl.CostEstimate(
            flops=2 * count * features * hidden,
            bytes_accessed=2 * count * features + 2 * features * hidden + 4 * count * width,
            transcendentals=0,
        ),
        name="grad_hidden",
    )(rows, down, bias)


def expert_kernel(
    features,
    experts,
    rows_ref,
    first_ref,
    gate_ref,
    up_ref,
    gate_bias_ref,
    up_bias_ref,
    mine_ref,
    grad_rows_ref,
    act_ref,
    act_gated_ref,
    grad_gate_ref,
    grad_up_ref,
    bias_sums_ref,
):
    hidden = gate_ref.shape[0]
    rows = rows_ref[:, :features]
    mine = mine_ref[...]
    gate = jnp.sum(rows_ref[:, features:].astype(F32) * mine, axis=1, keepdims=True)
    gate_lin = dot(rows, gate_ref[...], NT) + gate_bias_ref[...]
    up_lin = dot(rows, up_ref[...], NT) + up_bias_ref[...]
    gate_tanh = jnp.tanh(gate_lin * (1.0 / CLAMP_LIMIT))
    up_tanh = jnp.tanh(up_lin * (1.0 / CLAMP_LIMIT))
    gate_soft = CLAMP_LIMIT * gate_tanh
    up_one = CLAMP_LIMIT * up_tanh + 1.0
    sigmoid = 1.0 / (1.0 + jnp.exp(-GLU_SLOPE * gate_soft))
    swish = gate_soft * sigmoid
    act = (up_one * swish).astype(LOW)
    act_ref[...] = act
    act_gated_ref[...] = (act.astype(F32) * gate).astype(LOW)
    first = first_ref[:, :hidden]
    with_bias = jnp.max(first_ref[:, hidden:], axis=1, keepdims=True)
    grad_weight = jnp.sum(act.astype(F32) * first, axis=1, keepdims=True) + with_bias
    grad_act = first * gate
    swish_slope = sigmoid + GLU_SLOPE * swish * (1.0 - sigmoid)
    grad_gate = (grad_act * up_one * swish_slope * (1.0 - gate_tanh * gate_tanh)).astype(LOW)
    grad_up = (grad_act * swish * (1.0 - up_tanh * up_tanh)).astype(LOW)
    grad_gate_ref[...] = grad_gate
    grad_up_ref[...] = grad_up
    grad_rows = dot(grad_gate, gate_ref[...]) + dot(grad_up, up_ref[...])
    grad_rows_ref[:, :features] = grad_rows.astype(LOW)
    high = grad_weight.astype(LOW).astype(F32)
    lanes = lane_index(mine.shape)
    spread = jnp.where(lanes < experts, high, grad_weight - high) * mine
    grad_rows_ref[:, features:] = spread.astype(LOW)
    sums = jnp.concatenate(
        [
            jnp.sum(grad_gate.astype(F32), axis=0, keepdims=True),
            jnp.sum(grad_up.astype(F32), axis=0, keepdims=True),
        ],
        axis=0,
    )
    is_first = pl.program_id(0) == 0
    bias_sums_ref[...] = jnp.where(is_first, 0.0, bias_sums_ref[...]) + sums


def expert_step(rows, first, gate, up, gate_bias, up_bias, mine, features, experts):
    count, width = rows.shape
    hidden = gate.shape[0]
    first_width = first.shape[1]
    block = count // 4

    def by_row(columns):
        return pl.BlockSpec((block, columns), lambda i: (i, 0))

    def whole(shape):
        return pl.BlockSpec(shape, lambda i: (0, 0))

    return pl.pallas_call(
        functools.partial(expert_kernel, features, experts),
        grid=(count // block,),
        out_shape=(
            jax.ShapeDtypeStruct((count, width), LOW),
            jax.ShapeDtypeStruct((count, hidden), LOW),
            jax.ShapeDtypeStruct((count, hidden), LOW),
            jax.ShapeDtypeStruct((count, hidden), LOW),
            jax.ShapeDtypeStruct((count, hidden), LOW),
            jax.ShapeDtypeStruct((2, hidden), F32),
        ),
        in_specs=[
            by_row(width),
            by_row(first_width),
            whole((hidden, features)),
            whole((hidden, features)),
            whole((1, hidden)),
            whole((1, hidden)),
            whole((1, width - features)),
        ],
        out_specs=(
            by_row(width),
            by_row(hidden),
            by_row(hidden),
            by_row(hidden),
            by_row(hidden),
            whole((2, hidden)),
        ),
        compiler_params=kernel_params(),
        cost_estimate=pl.CostEstimate(
            flops=8 * count * features * hidden,
            bytes_accessed=4 * count * width + 4 * features * hidden + 12 * count * hidden,
            transcendentals=3 * count * hidden,
        ),
        name="expert_step",
    )(rows, first, gate, up, gate_bias, up_bias, mine)


def exchange(rows, parts):
    count, width = rows.shape
    moved = lax.all_to_all(
        rows.reshape(parts, count // parts, width),
        "expert",
        split_axis=0,
        concat_axis=0,
        tiled=True,
    )
    return moved.reshape(count, width)


def tensor_sum(values, ring, to_low=lambda v: v.astype(LOW)):
    near = [(i, i ^ 1) for i in range(ring)]
    far = [(i, ring - 1 - i) for i in range(ring)]
    half = values.shape[0] // 2
    upper, lower = to_low(values[:half]), to_low(values[half:])
    upper_in = lax.ppermute(upper, "tensor", near)
    lower_in = lax.ppermute(lower, "tensor", far)
    upper = to_low(upper.astype(F32) + upper_in.astype(F32))
    lower = to_low(lower.astype(F32) + lower_in.astype(F32))
    upper_in = lax.ppermute(upper, "tensor", far)
    lower_in = lax.ppermute(lower, "tensor", near)
    return jnp.concatenate(
        [upper.astype(F32) + upper_in.astype(F32), lower.astype(F32) + lower_in.astype(F32)],
        axis=0,
    )


def on_device(
    expert_axis,
    tensor_axis,
    block_input,
    out_cotangent,
    seq_lengths,
    route_ids,
    attn_gain,
    w_query,
    w_key,
    w_value,
    b_query,
    b_key,
    b_value,
    sink_logits,
    w_output,
    b_output,
    ffn_gain,
    w_router,
    b_router,
    w_gate,
    w_up,
    b_gate,
    b_up,
    w_down,
    b_down,
):
    tokens, features = block_input.shape
    heads = sink_logits.shape[0]
    experts = w_router.shape[1]
    capacity = 2 * tokens * route_ids.shape[1] // experts
    slots = experts * capacity
    shard = w_query.shape[0]
    shard_pad = round_up(shard + 1, 16)
    qkv_width = w_query.shape[1] + w_key.shape[1] + w_value.shape[1]
    width = round_up(features + 2 * experts, 128)
    mine_expert = lax.axis_index("expert")
    mine_tensor = lax.axis_index("tensor")

    packed = jnp.concatenate([w_query, w_key, w_value, w_output.T], axis=1)
    packed = jnp.pad(packed, ((0, shard_pad - shard), (0, 0)))
    weights = lax.all_gather(packed, "expert", axis=0, tiled=True)

    expert_ids = jnp.arange(experts, dtype=jnp.int32)
    named = jnp.any(route_ids[:, :, None] == expert_ids[None, None, :], axis=1)
    named_t = jnp.any(route_ids.T[:, None, :] == expert_ids[None, :, None], axis=0)
    token_ids = jnp.arange(tokens, dtype=jnp.int32)
    earlier = (token_ids[:, None] < token_ids[None, :]).astype(LOW)
    rank_t = dot(named_t.astype(LOW), earlier).astype(jnp.int32)
    place = (rank_t[:, None, :] == jnp.arange(capacity, dtype=jnp.int32)[None, :, None]) & named_t[
        :, None, :
    ]
    place = place.astype(LOW).reshape(slots, tokens)

    grad_rows_in = exchange(dot(place, out_cotangent).astype(LOW), experts)

    segment, position = layout(seq_lengths[0], tokens)
    cos, sin = rope_tables(position)
    allowed = (segment[:, None] == segment[None, :]) & (token_ids[None, :] <= token_ids[:, None])
    allowed = allowed.astype(F32)

    inputs = block_input.astype(F32)
    scale_one = lax.rsqrt(jnp.mean(inputs * inputs, axis=-1, keepdims=True) + EPSILON)
    unit_one = inputs * scale_one
    normed_low = (unit_one * attn_gain).astype(LOW)
    spread_low = jnp.pad(
        normed_low.reshape(tokens, expert_axis, shard), ((0, 0), (0, 0), (0, shard_pad - shard))
    )
    one_column = (jnp.arange(shard_pad) == shard).astype(LOW)
    sent_low = jnp.transpose(spread_low + one_column, (1, 0, 2))
    normed_all = exchange(sent_low.reshape(expert_axis * tokens, shard_pad), expert_axis)

    bias = jnp.concatenate([b_query, b_key, b_value])
    qkv = dot(spread_low.reshape(tokens, expert_axis * shard_pad), weights[:, :qkv_width]) + bias
    attn_low, rotated, lse = attend_forward(sink_logits, qkv, cos, sin, allowed)
    attn_all = lax.all_gather(attn_low, "expert", axis=0, tiled=True)

    def compact(padded):
        return padded.reshape(padded.shape[0], expert_axis, shard_pad)[:, :, :shard].reshape(
            padded.shape[0], features
        )

    attn_part = compact(dot(attn_low, weights[:, qkv_width:], NT))
    residual = inputs + tensor_sum(attn_part, tensor_axis) + b_output
    scale_two = lax.rsqrt(jnp.mean(residual * residual, axis=-1, keepdims=True) + EPSILON)
    unit_two = residual * scale_two
    normed_two = unit_two * ffn_gain
    logits = jnp.dot(normed_two, w_router, precision=PRECISE) + b_router
    gates = jax.nn.softmax(jnp.where(named, logits, MASKED), axis=-1)
    gates = jnp.where(named, gates, 0.0)

    gates_high, gates_low = split_low(gates)
    spare = width - features - 2 * experts
    sent = jnp.concatenate(
        [normed_two.astype(LOW), gates_high, gates_low, jnp.zeros((tokens, spare), LOW)], axis=1
    )
    rows_in = exchange(dot(place, sent).astype(LOW), experts)

    gate_t, up_t, down = w_gate[0].T, w_up[0].T, w_down[0]
    bias_once = jnp.where(mine_tensor == 0, b_down, 0.0)
    first = grad_hidden_product(grad_rows_in, down, bias_once)
    lane = jnp.arange(width - features)
    mine = ((lane % experts == mine_expert) & (lane < 2 * experts)).astype(F32)[None, :]
    grad_rows, act, act_gated, grad_gate, grad_up, bias_sums = expert_step(
        rows_in, first, gate_t, up_t, b_gate, b_up, mine, features, experts
    )
    grad_back = exchange(grad_rows, experts)

    result = (dot(act, down) + bias_once).astype(LOW)
    returned = exchange(result, experts)

    gate_column = jnp.sum(rows_in[:, features:].astype(F32) * mine, axis=1)
    w_down_grad = dot(act_gated, grad_rows_in, TN)[None]
    b_down_grad = dot(gate_column.astype(LOW)[None, :], grad_rows_in)
    w_gate_grad = dot(grad_gate, rows_in[:, :features], TN).T[None]
    w_up_grad = dot(grad_up, rows_in[:, :features], TN).T[None]
    b_gate_grad = bias_sums[0:1]
    b_up_grad = bias_sums[1:2]

    def resplit(values):
        main, spread = values[:, :features], values[:, features:]
        weight = spread[:, :experts] + spread[:, experts : 2 * experts]
        high, low = split_low(weight)
        return jnp.concatenate([main.astype(LOW), high, low], axis=1)

    back = tensor_sum(dot(place, grad_back, TN)[:, : features + 2 * experts], tensor_axis, resplit)
    grad_gates = back[:, features : features + experts] + back[:, features + experts :]
    grad_logits = gates * (grad_gates - jnp.sum(gates * grad_gates, axis=-1, keepdims=True))
    grad_two = back[:, :features] + jnp.dot(grad_logits, w_router.T, precision=PRECISE)
    cotangent = out_cotangent.astype(F32)
    scaled_two = grad_two * ffn_gain
    grad_resid = cotangent + scale_two * (
        scaled_two - unit_two * jnp.mean(unit_two * scaled_two, axis=-1, keepdims=True)
    )
    ffn_gain_part = jnp.sum(grad_two * unit_two, axis=0)
    router_part = jnp.dot(grad_logits.T, normed_two, precision=PRECISE)
    router_bias_part = jnp.sum(grad_logits, axis=0)
    output_bias_part = jnp.sum(grad_resid, axis=0)
    resid_low = grad_resid.astype(LOW)

    whole = weights.reshape(expert_axis, shard_pad, weights.shape[1])[:, :shard].reshape(
        features, weights.shape[1]
    )
    grad_attn = dot(resid_low, whole[:, qkv_width:]).astype(LOW)
    grad_qkv, sink_part = attend_backward(
        sink_logits, rotated, grad_attn, lse, cos, sin, allowed
    )
    grad_qkv_all = lax.all_gather(grad_qkv, "expert", axis=0, tiled=True)

    sent_resid = jnp.pad(
        resid_low.reshape(tokens, expert_axis, shard), ((0, 0), (0, 0), (0, shard_pad - shard))
    )
    sent_resid = jnp.transpose(sent_resid, (1, 0, 2)).reshape(expert_axis * tokens, shard_pad)
    resid_all = exchange(sent_resid, expert_axis)
    w_output_grad = dot(resid_all, attn_all, TN)[:shard].T

    grad_normed_part = dot(grad_qkv, whole[:, :qkv_width], NT)
    attn_gain_part = jnp.sum(grad_normed_part * unit_one, axis=0)

    last = jnp.concatenate([sink_part[0, :heads], router_bias_part])
    last = jnp.pad(last, (0, features - last.shape[0]))
    vectors = jnp.stack([attn_gain_part, ffn_gain_part, output_bias_part, last])
    vectors = jnp.transpose(vectors.reshape(4, expert_axis, shard), (1, 0, 2))
    vectors = vectors.reshape(expert_axis, 4 * shard)
    small = jnp.concatenate([router_part, vectors], axis=1).astype(LOW)
    small = lax.all_to_all(small, "expert", split_axis=0, concat_axis=0, tiled=True)
    small = jnp.sum(small.astype(F32), axis=0)
    gain_here = small[features : features + shard]
    near = [(i, i ^ 1) for i in range(tensor_axis)]
    far = [(i, tensor_axis - 1 - i) for i in range(tensor_axis)]
    gain_here = gain_here + lax.ppermute(gain_here, "tensor", near)
    gain_here = gain_here + lax.ppermute(gain_here, "tensor", far)
    small = jnp.concatenate([small[:features], gain_here, small[features + shard :]])
    small = lax.all_gather(small.astype(LOW), "expert", axis=0).astype(F32)
    w_router_grad = small[:, :features].T
    vectors = jnp.transpose(small[:, features:].reshape(expert_axis, 4, shard), (1, 0, 2))
    vectors = vectors.reshape(4, features)

    grad_normed = tensor_sum(grad_normed_part, tensor_axis) * attn_gain
    input_grad = grad_resid + scale_one * (
        grad_normed - unit_one * jnp.mean(unit_one * grad_normed, axis=-1, keepdims=True)
    )

    weighted = place.reshape(experts, capacity, tokens).astype(F32) * gates.T[:, None, :]
    weighted = weighted.astype(LOW).reshape(slots, tokens)
    mixed = tensor_sum(dot(weighted, returned, TN), tensor_axis)
    block_output = (residual + mixed).astype(LOW)

    qkv_grad = dot(normed_all, grad_qkv_all, TN)
    query_end = w_query.shape[1]
    key_end = query_end + w_key.shape[1]
    return (
        block_output,
        input_grad,
        vectors[0],
        qkv_grad[:shard, :query_end],
        qkv_grad[:shard, query_end:key_end],
        qkv_grad[:shard, key_end:],
        qkv_grad[shard, :query_end],
        qkv_grad[shard, query_end:key_end],
        qkv_grad[shard, key_end:],
        vectors[3, :heads],
        w_output_grad,
        vectors[2],
        vectors[1],
        w_router_grad,
        vectors[3, heads : heads + experts],
        w_gate_grad,
        w_up_grad,
        b_gate_grad,
        b_up_grad,
        w_down_grad,
        b_down_grad,
    )


def solution(mesh):
    in_specs = (
        P("expert", None),
        P("expert", None),
        P("expert", None),
        P("expert", None),
        P(),
        P("expert", "tensor"),
        P("expert", "tensor"),
        P("expert", "tensor"),
        P("tensor"),
        P("tensor"),
        P("tensor"),
        P("tensor"),
        P("tensor", "expert"),
        P(),
        P(),
        P(),
        P(),
        P("expert", None, "tensor"),
        P("expert", None, "tensor"),
        P("expert", "tensor"),
        P("expert", "tensor"),
        P("expert", "tensor", None),
        P("expert", None),
    )
    out_specs = (
        P("expert", None),
        P("expert", None),
        P(),
        P("expert", "tensor"),
        P("expert", "tensor"),
        P("expert", "tensor"),
        P("tensor"),
        P("tensor"),
        P("tensor"),
        P("tensor"),
        P("tensor", "expert"),
        P(),
        P(),
        P(),
        P(),
        P("expert", None, "tensor"),
        P("expert", None, "tensor"),
        P("expert", "tensor"),
        P("expert", "tensor"),
        P("expert", "tensor", None),
        P("expert", None),
    )
    body = functools.partial(on_device, mesh.shape["expert"], mesh.shape["tensor"])
    return jax.shard_map(body, mesh=mesh, in_specs=in_specs, out_specs=out_specs, check_vma=False)
```

time: 1390 us -> 717 us (0.52)
  blocking collectives: 638 us -> 29.5 us
  local copies, waits for them, and re-layouts: 127 us -> 74.2 us
  Pallas kernels: 0 us -> 51.2 us
  matrix products: 145 us -> 98 us
  other arithmetic: 63.5 us -> 29 us
  starting transfers between devices: 40.2 us -> 69.7 us
    psum x2 -> x0, blocking collectives: 495 us -> none  [the longest x1 369 us: to_sources(): summed = lax.psum(partial_rows, 'tensor')]
    psum x4 -> x0, waiting for transfers between devices: 133 us -> none  [the longest x1 68.1 us: on_device(): lax.psum(router_part.astype(jnp.bfloat16), 'expert').astype(jnp.float32)]
    unnamed x1 -> x0, blocking collectives: 92.5 us -> none
    all_gather x2 -> x3, waiting for transfers between devices: 34.5 us -> 95.9 us  [the longest x1 95.9 us: on_device(): weights = lax.all_gather(packed, 'expert', axis=0, tiled=True)]
    pallas_call x0 -> x4, Pallas kernels: none -> 51.2 us  [the longest x1 27.2 us: expert_step(): pl.pallas_call(functools.partial(expert_kernel, features, experts), grid=...]
    dot_general x34 -> x17, matrix products: 139 us -> 94.7 us  [the longest x16 93 us: dot(): return lax.dot_general(left, right, dims, preferred_element_type=F32)]
    ppermute x0 -> x18, waiting for transfers between devices: none -> 36.2 us  [the longest x4 12 us: tensor_sum(): upper_in = lax.ppermute(upper, 'tensor', far)]
    ppermute x0 -> x18, starting transfers between devices: none -> 28.6 us  [the longest x4 11.2 us: tensor_sum(): upper_in = lax.ppermute(upper, 'tensor', near)]
  transfers between devices with their start and end apart: 18 -> 28, of which waited for: 8 -> 15; matrix products, arithmetic and copies ran while one was open for 15% -> 24% of each run, Pallas kernels for 0% -> 3%
where the time goes in v1:
time: 717 us; the launch traced here: 710 us
  waiting for transfers between devices  343 us (48%)
  matrix products  98 us (14%)
  local copies, waits for them, and re-layouts  74.2 us (10%)
  starting transfers between devices  69.7 us (10%)
  Pallas kernels  51.2 us (7%)
  blocking collectives  29.5 us (4%)
  other arithmetic  29 us (4%)
  between operations  15.1 us (2%)
    all_to_all x6, waiting for transfers between devices, exchange(): lax.all_to_all(rows.reshape(parts, count // parts, width), 'expert', spli...  202 us
    all_gather x1, waiting for transfers between devices, on_device(): weights = lax.all_gather(packed, 'expert', axis=0, tiled=True)  95.9 us
    dot_general x16, matrix products, dot(): return lax.dot_general(left, right, dims, preferred_element_type=F32)  93 us
    all_to_all x6, starting transfers between devices, exchange(): lax.all_to_all(rows.reshape(parts, count // parts, width), 'expert', spli...  35 us
    all_gather x1, blocking collectives, on_device(): small = lax.all_gather(small.astype(LOW), 'expert', axis=0).astype(F32)  29.5 us
    pallas_call x1, Pallas kernels, expert_step(): pl.pallas_call(functools.partial(expert_kernel, features, experts), grid=...  27.2 us
  transfers between devices with their start and end apart: 28, of which 15 were waited for; matrix products, arithmetic and copies ran while one was open for 24% of the time, Pallas kernels for 3%

profile of v1, /device:TPU:32, one launch (start us, length us, event | category | flops | bytes accessed | tf_op | source)
XLA Modules:
  0.0 709.7 jit_solution(11966145660128043039)
XLA Ops:
  14.7 8.5 %copy.180 = bf16[1024,2880]{1,0:T(8,128)(2,1)} copy(bf16[1024,2880]{0,1:T(8,128)(2,1)} %convolution_convert_fusion) | data formatting | bytes 11796480 | tf_op jit(solution)/shard_map/convert_element_type | solution.py:445
  23.1 7.8 %all-to-all-start.1 = ((bf16[32,32,2880]{2,1,0:T(8,128)(2,1)}), bf16[32,32,2880]{2,1,0:T(8,128)(2,1)}, u32[]{:S(2)}, u32[]{:S(2)}) async-start(bf16[32,32,2880]{2,1,0:T(8,128)(2,1)} %bitcast.125), calls=%async_computation.1 | async-start | bytes 12058624 | tf_op jit(solution)/shard_map/all_to_all | solution.py:364
  36.0 95.9 %all-gather.5.cloned.1.call-done = bf16[3072,2304]{1,0:T(8,128)(2,1)} async-done(((bf16[96,2304]{1,0:T(8,128)(2,1)}), bf16[3072,2304]{1,0:T(8,128)(2,1)}) %all-gather.5.cloned.1.call-update) | async-done | bytes 14155792 | tf_op jit(solution)/shard_map/all_gather | solution.py:432
  131.9 5.3 fusion.15.qkv_ref
  137.2 7.4 %attend_forward.1 = (bf16[128,1024]{1,0:T(8,128)(2,1)}, bf16[128,1280]{1,0:T(8,128)(2,1)}, f32[128,128]{1,0:T(8,128)}) custom-call(f32[16]{0:T(128)} %sink_ref.3, f32[128,1280]{1,0:T(8,128)} %fusion.15.qkv_ref, f32[128,128]{1,0:T(8,128)} %get-tuple-element.127.cos_ref, f32[128,128]{1,0:T(8,128)} %get-tuple-element.128.sin_ref, f32[128,128]{1,0:T(8,128)} %fusion.75.allowed_ref), custom_call_target="tpu_custom_call" | custom-call | tf_op jit(solution)/shard_map/attend_forward/pallas_call | solution.py:191
  159.8 5.2 collective-permute-done.2
  170.8 6.0 collective-permute-done.3
  185.7 5.4 convolution_convert_fusion.1
  191.1 6.9 all-to-all-start
  199.2 9.6 %grad_hidden.1.first_ref = f32[1024,768]{1,0:T(8,128)} custom-call(bf16[1024,2880]{1,0:T(8,128)(2,1)} %bitcast.14.rows_ref, bf16[720,2880]{1,0:T(8,128)(2,1)} %bitcast.146, f32[1,2880]{1,0:T(1,128)} %get-tuple-element.94.bias_ref), custom_call_target="tpu_custom_call" | custom-call | flops 4246732800 | bytes 13191168 | tf_op jit(solution)/shard_map/grad_hidden/pallas_call | solution.py:234
  208.8 63.9 %all-to-all-done = bf16[32,32,2944]{2,1,0:T(8,128)(2,1)} async-done(((bf16[32,32,2944]{2,1,0:T(8,128)(2,1)}), bf16[32,32,2944]{2,1,0:T(8,128)(2,1)}, u32[]{:S(2)}, u32[]{:S(2)}) %all-to-all-start) | async-done | bytes 6029344 | tf_op jit(solution)/shard_map/all_to_all | solution.py:364
  272.7 27.2 %expert_step.1 = (bf16[1024,2944]{1,0:T(8,128)(2,1)}, bf16[1024,720]{1,0:T(8,128)(2,1)}, bf16[1024,720]{1,0:T(8,128)(2,1)}, bf16[1024,720]{1,0:T(8,128)(2,1)}, b...) custom-call(bf16[1024,2944]{1,0:T(8,128)(2,1)} %bitcast.12.rows_ref, f32[1024,768]{1,0:T(8,128)} %grad_hidden.1.first_ref, ...), custom_call_target="tpu_custom_call" | custom-call | flops 16986931200 | bytes 29200384 | tf_op jit(solution)/shard_map/expert_step/pallas_call | solution.py:324
  299.9 10.1 %add_convert_fusion = bf16[1024,2880]{0,1:T(8,128)(2,1)} fusion(f32[2880]{0:T(1024)S(1)} %get-tuple-element.93, bf16[1024,720]{1,0:T(8,128)(2,1)} %get-tuple-element.33, bf16[1,720,2880]{2,1,0:T(8,128)(2,1)} %param.44), kind=kOutput, calls=%fused_computation | convolution fusion | flops 4252631040 | bytes 11531520 | tf_op jit(solution)/shard_map/dot_general | solution.py:31
  310.0 8.5 %copy.181 = bf16[1024,2880]{1,0:T(8,128)(2,1)} copy(bf16[1024,2880]{0,1:T(8,128)(2,1)} %add_convert_fusion) | data formatting | bytes 11796480 | tf_op jit(solution)/shard_map/convert_element_type | solution.py:499
  324.1 79.5 %all-to-all-done.2 = bf16[32,32,2880]{2,1,0:T(8,128)(2,1)} async-done(((bf16[32,32,2880]{2,1,0:T(8,128)(2,1)}), bf16[32,32,2880]{2,1,0:T(8,128)(2,1)}, u32[]{:S(2)}, u32[]{:S(2)}) %all-to-all-start.2) | async-done | bytes 5898272 | tf_op jit(solution)/shard_map/all_to_all | solution.py:364
  403.6 5.1 all-to-all-start.3
  410.1 13.3 %reshape.337 = bf16[2880,2304]{1,0:T(8,128)(2,1)} reshape(bf16[32,90,2304]{2,1,0:T(8,128)(2,1)} %bitcast.127) | data formatting | bytes 26542080 | tf_op jit(solution)/shard_map/reshape | solution.py:531
  428.3 5.4 collective-permute-start.4
  433.8 56.7 %all-to-all-done.3 = bf16[32,32,2944]{2,1,0:T(8,128)(2,1)} async-done(((bf16[32,32,2944]{2,1,0:T(8,128)(2,1)}), bf16[32,32,2944]{2,1,0:T(8,128)(2,1)}, u32[]{:S(2)}, u32[]{:S(2)}) %all-to-all-start.3) | async-done | bytes 6029344 | tf_op jit(solution)/shard_map/all_to_all | solution.py:364
  529.4 5.1 fusion.36.grad_ref
  534.5 7.0 attend_backward.1
  547.1 10.5 %convolution_bitcast_fusion.2 = f32[1,2880,720]{1,2,0:T(8,128)} fusion(bf16[1024,720]{1,0:T(8,128)(2,1)S(1)} %copy-done.47, bf16[1024,2944]{1,0:T(8,128)(2,1)} %bitcast.12.rows_ref), kind=kOutput, calls=%fused_computation.13 | convolution fusion | flops 4246732800 | bytes 15798272 | tf_op jit(solution)/shard_map/dot_general | solution.py:31
  557.6 10.2 %convolution_bitcast_fusion.1 = f32[1,2880,720]{1,2,0:T(8,128)} fusion(bf16[1024,720]{1,0:T(8,128)(2,1)S(1)} %copy-done.46, bf16[1024,2944]{1,0:T(8,128)(2,1)} %bitcast.12.rows_ref), kind=kOutput, calls=%fused_computation.12 | convolution fusion | flops 4246732800 | bytes 15798272 | tf_op jit(solution)/shard_map/dot_general | solution.py:31
  567.8 10.1 %convolution_bitcast_fusion = f32[1,720,2880]{2,1,0:T(8,128)} fusion(bf16[1024,720]{1,0:T(8,128)(2,1)S(1)} %copy-done.45, bf16[1024,2880]{1,0:T(8,128)(2,1)} %bitcast.14.rows_ref), kind=kOutput, calls=%fused_computation.11 | convolution fusion | flops 4246732800 | bytes 15667200 | tf_op jit(solution)/shard_map/dot_general | solution.py:31
  583.7 9.0 %collective-permute-done.12 = bf16[64,2880]{1,0:T(8,128)(2,1)S(1)} collective-permute-done((bf16[64,2880]{1,0:T(8,128)(2,1)S(1)}, bf16[64,2880]{1,0:T(8,128)(2,1)S(1)}, u32[]{:S(2)}, u32[]{:S(2)}) %collective-permute-start.12) | collective-permute-done | bytes 368672 | tf_op jit(solution)/shard_map/ppermute | solution.py:379
  604.6 6.3 collective-permute-done.13
  614.4 5.8 all-to-all-start.4
  620.2 8.4 %all-to-all-done.4 = bf16[32,2,1620]{2,1,0:T(2,128)(2,1)} async-done(((bf16[32,2,1620]{2,1,0:T(2,128)(2,1)}), bf16[32,2,1620]{2,1,0:T(2,128)(2,1)}, u32[]{:S(2)}, u32[]{:S(2)}) %all-to-all-start.4) | async-done | bytes 207392 | tf_op jit(solution)/shard_map/all_to_all | solution.py:556
  647.7 5.6 all-to-all-start.5
  654.8 29.5 %all-gather = bf16[32,1,3240]{2,1,0:T(2,128)(2,1)S(1)} all-gather(bf16[1,1,3240]{2,1,0:T(2,128)(2,1)S(1)} %bitcast.138), channel_id=1, replica_groups=mesh['expert'=32,'tensor'=4] {'expert'}, dimensions={0}, use_global_device_ids=true | all-gather | bytes 213840 | tf_op jit(solution)/shard_map/all_gather | solution.py:564
  688.8 5.6 convolution_bitcast_fusion.5
  694.4 5.8 fusion.48
  (284 shorter events, 148.0 us)
Async XLA Ops:
  7.2 172.8 %copy-start = (f32[2880,32]{0,1:T(8,128)S(1)}, f32[2880,32]{0,1:T(8,128)}, u32[]{:S(2)}) copy-start(f32[2880,32]{0,1:T(8,128)} %param.38) | copy-start | bytes 1105924
  7.2 124.6 %all-gather.5.cloned.1.call-start = ((), (), s32[]{:S(2)}) async-start(), calls=%async_computation.7 | async-start | bytes 14598144 | tf_op jit(solution)/shard_map/all_gather | solution.py:432
  23.1 168.0 %all-to-all-start.1 = ((bf16[32,32,2880]{2,1,0:T(8,128)(2,1)}), bf16[32,32,2880]{2,1,0:T(8,128)(2,1)}, u32[]{:S(2)}, u32[]{:S(2)}) async-start(bf16[32,32,2880]{2,1,0:T(8,128)(2,1)} %bitcast.125), calls=%async_computation.1 | async-start | bytes 12058624 | tf_op jit(solution)/shard_map/all_to_all | solution.py:364
  153.9 11.1 %collective-permute-start.2 = (bf16[64,2880]{1,0:T(8,128)(2,1)S(1)}, bf16[64,2880]{1,0:T(8,128)(2,1)}, u32[]{:S(2)}, u32[]{:S(2)}) collective-permute-start(bf16[64,2880]{1,0:T(8,128)(2,1)S(1)} %convert_element_type.309), channel_id=1, source_target_pairs={{0,3},{1,2},{2,1},{3,0},{4,7},{5,6},{6,5},{7,4},{8,11},{9,10},{10,... | collective-permute-start | bytes 1105928 | tf_op jit(solution)/shard_map/ppermute | solution.py:380
  157.6 11.4 %collective-permute-start = (bf16[64,2880]{1,0:T(8,128)(2,1)S(1)}, bf16[64,2880]{1,0:T(8,128)(2,1)S(1)}, u32[]{:S(2)}, u32[]{:S(2)}) collective-permute-start(bf16[64,2880]{1,0:T(8,128)(2,1)S(1)} %convert_element_type.303), channel_id=1, source_target_pairs={{0,1},{1,0},{2,3},{3,2},{4,5},{5,4},{6,7},{7,6},{8,9},{9,8},{10,11... | collective-permute-start | bytes 1105928 | tf_op jit(solution)/shard_map/ppermute | solution.py:379
  166.1 10.7 %collective-permute-start.3 = (bf16[64,2880]{1,0:T(8,128)(2,1)S(1)}, bf16[64,2880]{1,0:T(8,128)(2,1)S(1)}, u32[]{:S(2)}, u32[]{:S(2)}) collective-permute-start(bf16[64,2880]{1,0:T(8,128)(2,1)S(1)} %add_convert_fusion.5), channel_id=1, source_target_pairs={{0,1},{1,0},{2,3},{3,2},{4,5},{5,4},{6,7},{7,6},{8,9},{9,8},{10,11... | collective-permute-start | bytes 1105928 | tf_op jit(solution)/shard_map/ppermute | solution.py:384
  169.1 10.4 %collective-permute-start.1 = (bf16[64,2880]{1,0:T(8,128)(2,1)S(1)}, bf16[64,2880]{1,0:T(8,128)(2,1)S(1)}, u32[]{:S(2)}, u32[]{:S(2)}) collective-permute-start(bf16[64,2880]{1,0:T(8,128)(2,1)S(1)} %add_convert_fusion.6), channel_id=1, source_target_pairs={{0,3},{1,2},{2,1},{3,0},{4,7},{5,6},{6,5},{7,4},{8,11},{9,10},{10,... | collective-permute-start | bytes 1105928 | tf_op jit(solution)/shard_map/ppermute | solution.py:383
  191.1 81.6 %all-to-all-start = ((bf16[32,32,2944]{2,1,0:T(8,128)(2,1)}), bf16[32,32,2944]{2,1,0:T(8,128)(2,1)}, u32[]{:S(2)}, u32[]{:S(2)}) async-start(bf16[32,32,2944]{2,1,0:T(8,128)(2,1)} %bitcast.124), calls=%async_computation | async-start | bytes 12058624 | tf_op jit(solution)/shard_map/all_to_all | solution.py:364
  318.4 85.2 %all-to-all-start.2 = ((bf16[32,32,2880]{2,1,0:T(8,128)(2,1)}), bf16[32,32,2880]{2,1,0:T(8,128)(2,1)}, u32[]{:S(2)}, u32[]{:S(2)}) async-start(bf16[32,32,2880]{2,1,0:T(8,128)(2,1)} %bitcast.126), calls=%async_computation.2 | async-start | bytes 12058624 | tf_op jit(solution)/shard_map/all_to_all | solution.py:364
  323.3 365.5 %all-gather.9.cloned.1.call-start = ((), (), s32[]{:S(2)}) async-start(), calls=%async_computation.9 | async-start | bytes 8650752 | tf_op jit(solution)/shard_map/all_gather | solution.py:466
  403.6 86.8 %all-to-all-start.3 = ((bf16[32,32,2944]{2,1,0:T(8,128)(2,1)}), bf16[32,32,2944]{2,1,0:T(8,128)(2,1)}, u32[]{:S(2)}, u32[]{:S(2)}) async-start(bf16[32,32,2944]{2,1,0:T(8,128)(2,1)} %bitcast.131), calls=%async_computation.3 | async-start | bytes 12058624 | tf_op jit(solution)/shard_map/all_to_all | solution.py:364
  408.7 285.7 %all-gather.7.cloned.1.call-start = ((), (), s32[]{:S(2)}) async-start(), calls=%async_computation.8 | async-start | bytes 10813440 | tf_op jit(solution)/shard_map/all_gather | solution.py:538
  428.3 73.9 %collective-permute-start.4 = (bf16[64,2880]{1,0:T(8,128)(2,1)}, bf16[64,2880]{1,0:T(8,128)(2,1)}, u32[]{:S(2)}, u32[]{:S(2)}) collective-permute-start(bf16[64,2880]{1,0:T(8,128)(2,1)} %get-tuple-element.110), channel_id=1, source_target_pairs={{0,1},{1,0},{2,3},{3,2},{4,5},{5,4},{6,7},{7,6},{8,9},{9,8},{10,11... | collective-permute-start | bytes 1105928 | tf_op jit(solution)/shard_map/ppermute | solution.py:379
  433.8 68.5 %collective-permute-start.6 = (bf16[64,2880]{1,0:T(8,128)(2,1)}, bf16[64,2880]{1,0:T(8,128)(2,1)}, u32[]{:S(2)}, u32[]{:S(2)}) collective-permute-start(bf16[64,2880]{1,0:T(8,128)(2,1)} %get-tuple-element.111), channel_id=1, source_target_pairs={{0,3},{1,2},{2,1},{3,0},{4,7},{5,6},{6,5},{7,4},{8,11},{9,10},{10,... | collective-permute-start | bytes 1105928 | tf_op jit(solution)/shard_map/ppermute | solution.py:380
  497.0 10.9 %collective-permute-start.10 = (bf16[64,2944]{1,0:T(8,128)(2,1)}, bf16[64,2944]{1,0:T(8,128)(2,1)}, u32[]{:S(2)}, u32[]{:S(2)}) collective-permute-start(bf16[64,2944]{1,0:T(8,128)(2,1)} %concatenate.86), channel_id=1, source_target_pairs={{0,3},{1,2},{2,1},{3,0},{4,7},{5,6},{6,5},{7,4},{8,11},{9,10},{10,... | collective-permute-start | bytes 1130504 | tf_op jit(solution)/shard_map/ppermute | solution.py:380
  500.2 15.6 %collective-permute-start.8 = (bf16[64,2944]{1,0:T(8,128)(2,1)}, bf16[64,2944]{1,0:T(8,128)(2,1)}, u32[]{:S(2)}, u32[]{:S(2)}) collective-permute-start(bf16[64,2944]{1,0:T(8,128)(2,1)} %concatenate.84), channel_id=1, source_target_pairs={{0,1},{1,0},{2,3},{3,2},{4,5},{5,4},{6,7},{7,6},{8,9},{9,8},{10,11... | collective-permute-start | bytes 1130504 | tf_op jit(solution)/shard_map/ppermute | solution.py:379
  504.4 14.5 %collective-permute-start.7 = (bf16[64,2880]{1,0:T(8,128)(2,1)}, bf16[64,2880]{1,0:T(8,128)(2,1)}, u32[]{:S(2)}, u32[]{:S(2)}) collective-permute-start(bf16[64,2880]{1,0:T(8,128)(2,1)} %get-tuple-element.109), channel_id=1, source_target_pairs={{0,1},{1,0},{2,3},{3,2},{4,5},{5,4},{6,7},{7,6},{8,9},{9,8},{10,11... | collective-permute-start | bytes 1105928 | tf_op jit(solution)/shard_map/ppermute | solution.py:384
  504.5 15.6 %collective-permute-start.5 = (bf16[64,2880]{1,0:T(8,128)(2,1)}, bf16[64,2880]{1,0:T(8,128)(2,1)}, u32[]{:S(2)}, u32[]{:S(2)}) collective-permute-start(bf16[64,2880]{1,0:T(8,128)(2,1)} %get-tuple-element.108), channel_id=1, source_target_pairs={{0,3},{1,2},{2,1},{3,0},{4,7},{5,6},{6,5},{7,4},{8,11},{9,10},{10,... | collective-permute-start | bytes 1105928 | tf_op jit(solution)/shard_map/ppermute | solution.py:383
  510.9 11.3 %collective-permute-start.11 = (bf16[64,2944]{1,0:T(8,128)(2,1)S(1)}, bf16[64,2944]{1,0:T(8,128)(2,1)}, u32[]{:S(2)}, u32[]{:S(2)}) collective-permute-start(bf16[64,2944]{1,0:T(8,128)(2,1)S(1)} %concatenate.87), channel_id=1, source_target_pairs={{0,1},{1,0},{2,3},{3,2},{4,5},{5,4},{6,7},{7,6},{8,9},{9,8},{10,11... | collective-permute-start | bytes 1130504 | tf_op jit(solution)/shard_map/ppermute | solution.py:384
  518.8 7.7 %collective-permute-start.9 = (bf16[64,2944]{1,0:T(8,128)(2,1)S(1)}, bf16[64,2944]{1,0:T(8,128)(2,1)S(1)}, u32[]{:S(2)}, u32[]{:S(2)}) collective-permute-start(bf16[64,2944]{1,0:T(8,128)(2,1)S(1)} %concatenate.85), channel_id=1, source_target_pairs={{0,3},{1,2},{2,1},{3,0},{4,7},{5,6},{6,5},{7,4},{8,11},{9,10},{10,... | collective-permute-start | bytes 1130504 | tf_op jit(solution)/shard_map/ppermute | solution.py:383
  557.6 20.3 %slice-start = ((s8[13271040]{0:T(1024)(128)(4,1)}), s8[4194304]{0:T(1024)(128)(4,1)S(1)}, s32[]{:S(2)}) async-start(s8[13271040]{0:T(1024)(128)(4,1)} %bitcast.128), calls=%async_computation.10 | async-start | bytes 8388608
  557.6 20.3 %slice-start.1 = ((s8[13271040]{0:T(1024)(128)(4,1)}), s8[4194304]{0:T(1024)(128)(4,1)S(1)}, s32[]{:S(2)}) async-start(s8[13271040]{0:T(1024)(128)(4,1)} %bitcast.128), calls=%async_computation.11 | async-start | bytes 8388608
  581.7 11.1 %collective-permute-start.12 = (bf16[64,2880]{1,0:T(8,128)(2,1)S(1)}, bf16[64,2880]{1,0:T(8,128)(2,1)S(1)}, u32[]{:S(2)}, u32[]{:S(2)}) collective-permute-start(bf16[64,2880]{1,0:T(8,128)(2,1)S(1)} %get-tuple-element.104), channel_id=1, source_target_pairs={{0,1},{1,0},{2,3},{3,2},{4,5},{5,4},{6,7},{7,6},{8,9},{9,8},{10,11... | collective-permute-start | bytes 1105928 | tf_op jit(solution)/shard_map/ppermute | solution.py:379
  583.1 9.7 %collective-permute-start.14 = (bf16[64,2880]{1,0:T(8,128)(2,1)S(1)}, bf16[64,2880]{1,0:T(8,128)(2,1)S(1)}, u32[]{:S(2)}, u32[]{:S(2)}) collective-permute-start(bf16[64,2880]{1,0:T(8,128)(2,1)S(1)} %get-tuple-element.105), channel_id=1, source_target_pairs={{0,3},{1,2},{2,1},{3,0},{4,7},{5,6},{6,5},{7,4},{8,11},{9,10},{10,... | collective-permute-start | bytes 1105928 | tf_op jit(solution)/shard_map/ppermute | solution.py:380
  593.8 9.4 %collective-permute-start.15 = (bf16[64,2880]{1,0:T(8,128)(2,1)}, bf16[64,2880]{1,0:T(8,128)(2,1)}, u32[]{:S(2)}, u32[]{:S(2)}) collective-permute-start(bf16[64,2880]{1,0:T(8,128)(2,1)} %get-tuple-element.103), channel_id=1, source_target_pairs={{0,1},{1,0},{2,3},{3,2},{4,5},{5,4},{6,7},{7,6},{8,9},{9,8},{10,11... | collective-permute-start | bytes 1105928 | tf_op jit(solution)/shard_map/ppermute | solution.py:384
  602.9 7.9 %collective-permute-start.13 = (bf16[64,2880]{1,0:T(8,128)(2,1)S(1)}, bf16[64,2880]{1,0:T(8,128)(2,1)S(1)}, u32[]{:S(2)}, u32[]{:S(2)}) collective-permute-start(bf16[64,2880]{1,0:T(8,128)(2,1)S(1)} %copy-done.11), channel_id=1, source_target_pairs={{0,3},{1,2},{2,1},{3,0},{4,7},{5,6},{6,5},{7,4},{8,11},{9,10},{10,... | collective-permute-start | bytes 1105928 | tf_op jit(solution)/shard_map/ppermute | solution.py:383
  614.4 24.2 %copy-start.2 = (f32[128,2880]{1,0:T(8,128)S(1)}, f32[128,2880]{1,0:T(8,128)}, u32[]{:S(2)}) copy-start(f32[128,2880]{1,0:T(8,128)} %copy-done.1) | copy-start | bytes 4423684
  614.4 14.2 %all-to-all-start.4 = ((bf16[32,2,1620]{2,1,0:T(2,128)(2,1)}), bf16[32,2,1620]{2,1,0:T(2,128)(2,1)}, u32[]{:S(2)}, u32[]{:S(2)}) async-start(bf16[32,2,1620]{2,1,0:T(2,128)(2,1)} %reshape.370), calls=%async_computation.4 | async-start | bytes 425984 | tf_op jit(solution)/shard_map/all_to_all | solution.py:556
  628.5 19.2 %all-to-all-start.6 = ((bf16[32,128,96]{1,2,0:T(8,128)(2,1)}), bf16[32,128,96]{1,2,0:T(8,128)(2,1)}, u32[]{:S(2)}, u32[]{:S(2)}) async-start(bf16[32,128,96]{1,2,0:T(8,128)(2,1)} %pad_bitcast_fusion), calls=%async_computation.6 | async-start | bytes 1572864 | tf_op jit(solution)/shard_map/all_to_all | solution.py:364
  637.1 7.2 %collective-permute-start.16 = (f32[90]{0:T(128)S(1)}, f32[90]{0:T(128)S(1)}, u32[]{:S(2)}, u32[]{:S(2)}) collective-permute-start(f32[90]{0:T(128)S(1)} %slice.261), channel_id=1, source_target_pairs={{0,1},{1,0},{2,3},{3,2},{4,5},{5,4},{6,7},{7,6},{8,9},{9,8},{10,11... | collective-permute-start | bytes 1088 | tf_op jit(solution)/shard_map/ppermute | solution.py:561
  644.3 10.4 %collective-permute-start.17 = (f32[90]{0:T(128)S(1)}, f32[90]{0:T(128)S(1)}, u32[]{:S(2)}, u32[]{:S(2)}) collective-permute-start(f32[90]{0:T(128)S(1)} %slice_add_fusion.4), channel_id=1, source_target_pairs={{0,3},{1,2},{2,1},{3,0},{4,7},{5,6},{6,5},{7,4},{8,11},{9,10},{10,... | collective-permute-start | bytes 1088 | tf_op jit(solution)/shard_map/ppermute | solution.py:562
  647.7 46.7 %all-to-all-start.5 = ((bf16[32,128,96]{1,2,0:T(8,128)(2,1)}), bf16[32,128,96]{1,2,0:T(8,128)(2,1)S(1)}, u32[]{:S(2)}, u32[]{:S(2)}) async-start(bf16[32,128,96]{1,2,0:T(8,128)(2,1)} %get-tuple-element.98), calls=%async_computation.5 | async-start | bytes 1572864 | tf_op jit(solution)/shard_map/all_to_all | solution.py:364
  (48 other events, 267.5 us)
Sparse Core Ops, SparseCore 0:
  10.9 120.9 all-gather.4
  326.4 141.7 all-gather.8
  541.6 55.8 all-gather.6
